TPU v7x, 256 devices: a whole 4x4x8 slice. The times are simulated.
256 devices in a mesh: band: 32 (over y_hi, z, core), pw: 8 (over y_lo, x).
Axes of the slice: x: 4, y: 4 (y_hi: 2, y_lo: 2; y = y_hi * 2 + y_lo), z: 8, core: 2. Of those that a mesh axis runs over, the one named last changes fastest.
Arguments:
- orbitals: float32 [64, 128, 128, 128], P('band', 'pw'), may hold values from -6 to 6
- occupations: int32 [64], P('band'), may hold values from 1 to 2
Outputs:
- exchange_out: float32 [64, 128, 128, 128], P('band', 'pw')
All inputs are finite; a program needn't handle non-finite values.
Results may differ from a plain program's by a relative error of at most 0.000084.
Values sent between devices are 32-bit elements; how exact they have to be, the bound alone decides.
A program may use at most 128 MiB of HBM per device.

v0:
```python
import jax
import jax.numpy as jnp
import numpy as np
from jax import lax
from jax.sharding import PartitionSpec as P

MIXING = 0.25


def passed_along(value, axis, steps):
    count = lax.axis_size(axis)
    pairs = [(source, (source + steps) % count) for source in range(count)]
    return lax.ppermute(value, axis, pairs)


def basis(length):
    half = length // 2
    grid = np.arange(length)
    columns, waves = [], []
    for k in range(half + 1):
        scale = np.sqrt((1.0 if k in (0, half) else 2.0) / length)
        columns.append(scale * np.cos(2.0 * np.pi * (k * grid % length) / length))
        waves.append(k)
    for k in range(1, half):
        scale = np.sqrt(2.0 / length)
        columns.append(scale * np.sin(2.0 * np.pi * (k * grid % length) / length))
        waves.append(k)
    return np.stack(columns, axis=1).astype(np.float32), np.array(waves)


def apply_table(form, field, table):
    return jnp.einsum(form, field, table, precision=lax.Precision.HIGH)


def shards(orbitals, occupations):
    count = orbitals.shape[0]
    slab_x, full_y, full_z = (orbitals.shape[1], orbitals.shape[2], orbitals.shape[3])
    groups = lax.axis_size("pw")
    full_x = slab_x * groups
    slab_y = full_y // groups
    table_x, waves_x = basis(full_x)
    table_y, waves_y = basis(full_y)
    table_z, waves_z = basis(full_z)
    weights = occupations.astype(jnp.float32) * 0.5
    passing, passing_weights = passed_along((orbitals, weights), "band", 1)
    densities = (orbitals[:, None] * passing[None, :]).reshape(
        (count * count, slab_x, full_y, full_z)
    )
    field = apply_table("pxyn,nk->pxyk", densities, table_z)
    field = apply_table("pxny,nk->pxky", field, table_y)
    start_y = lax.axis_index("pw") * slab_y
    wave_x = jnp.asarray(waves_x * (2.0 * np.pi / full_x), jnp.float32)
    wave_y = lax.dynamic_slice_in_dim(
        jnp.asarray(waves_y * (2.0 * np.pi / full_y), jnp.float32), start_y, slab_y
    )
    wave_z = jnp.asarray(waves_z * (2.0 * np.pi / full_z), jnp.float32)
    square = (
        wave_x[:, None, None] * wave_x[:, None, None]
        + wave_y[None, :, None] * wave_y[None, :, None]
        + wave_z[None, None, :] * wave_z[None, None, :]
    )
    safe = jnp.where(square > 0, square, 1.0)
    coulomb = jnp.where(square > 0, 4.0 * jnp.pi / safe, 0.0)
    field = lax.all_to_all(field, "pw", split_axis=2, concat_axis=1, tiled=True)
    spectrum = apply_table("pnyz,nk->pkyz", field, table_x) * coulomb
    field = apply_table("pkyz,nk->pnyz", spectrum, table_x)
    field = lax.all_to_all(field, "pw", split_axis=1, concat_axis=2, tiled=True)
    field = apply_table("pxky,nk->pxny", field, table_y)
    potential = apply_table("pxyk,nk->pxyn", field, table_z)
    potential = potential.reshape((count, count, slab_x, full_y, full_z))
    theirs = jnp.sum(
        potential * ((-MIXING * weights)[:, None, None, None] * orbitals)[:, None], axis=0
    )
    returned = passed_along(theirs, "band", -1)
    own = jnp.sum(
        potential * ((-MIXING * passing_weights)[:, None, None, None] * passing)[None], axis=1
    )
    return own + returned


def solution(mesh):
    placed = (P("band", "pw", None, None), P("band"))
    return jax.shard_map(
        shards, mesh=mesh, in_specs=placed, out_specs=P("band", "pw", None, None), check_vma=False
    )
```

profile of v0, /device:TPU:71, one launch (start us, length us, event | category | flops | bytes accessed | tf_op | source)
XLA Modules:
  0.0 231.1 jit_solution(17152674087235560025)
XLA Ops:
  0.0 2.2 collective-permute-start
  2.2 23.3 %collective-permute-done = f32[2,16,128,128]{3,2,1,0:T(8,128)S(1)} collective-permute-done((f32[2,16,128,128]{3,2,1,0:T(8,128)}, f32[2,16,128,128]{3,2,1,0:T(8,128)S(1)}, u32[]{:S(2)}, u32[]{:S(2)}) %collective-permute-start) | collective-permute-done | bytes 2097184 | tf_op jit(solution)/shard_map/ppermute | solution.py:13
  25.5 2.8 %broadcast_multiply_fusion = f32[2,2,16,128,128]{4,3,2,1,0:T(8,128)S(1)} fusion(f32[2,16,128,128]{3,2,1,0:T(8,128)S(1)} %collective-permute-done, f32[2,16,128,128]{3,2,1,0:T(8,128)} %param.11), kind=kLoop, calls=%fused_computation.11 | loop fusion | flops 1048576 | bytes 8388608 | tf_op jit(solution)/shard_map/mul | solution.py:46
  28.4 1.9 fusion.9
  30.3 3.4 %convolution_bitcast_fusion = f32[4,16,128,128]{2,3,1,0:T(8,128)} fusion(f32[4,16,128,128]{2,3,1,0:T(8,128)S(1)} %fusion.9, f32[128,128,1,1]{1,0,3,2:T(8,128)S(1)} %copy-done.4), kind=kOutput, calls=%fused_computation.9 | convolution fusion | flops 805306368 | bytes 8454144 | tf_op jit(solution)/shard_map/pxny,nk->pxky/dot_general | solution.py:32
  33.7 5.5 %copy.16 = f32[4,16,128,128]{3,1,0,2:T(8,128)} copy(f32[4,16,128,128]{2,3,1,0:T(8,128)} %convolution_bitcast_fusion) | data formatting | bytes 8388608 | tf_op jit(solution)/shard_map/pxny,nk->pxky/transpose | solution.py:32
  39.2 5.4 %all-to-all-start = ((f32[4,16,128,128]{3,1,0,2:T(8,128)}), f32[4,16,128,128]{3,1,0,2:T(8,128)}, u32[]{:S(2)}, u32[]{:S(2)}) async-start(f32[4,16,128,128]{3,1,0,2:T(8,128)} %copy.16), calls=%async_computation | async-start | bytes 8388608 | tf_op jit(solution)/shard_map/all_to_all | solution.py:64
  45.0 59.6 %all-to-all-done = f32[4,16,128,128]{3,1,0,2:T(8,128)} async-done(((f32[4,16,128,128]{3,1,0,2:T(8,128)}), f32[4,16,128,128]{3,1,0,2:T(8,128)}, u32[]{:S(2)}, u32[]{:S(2)}) %all-to-all-start) | async-done | bytes 4194336 | tf_op jit(solution)/shard_map/all_to_all | solution.py:64
  104.6 4.6 %copy.17 = f32[4,16,128,128]{3,2,1,0:T(8,128)S(1)} copy(f32[4,16,128,128]{3,1,0,2:T(8,128)} %all-to-all-done) | data formatting | bytes 8388608 | tf_op jit(solution)/shard_map/all_to_all | solution.py:64
  109.3 3.8 %fusion.3 = f32[4,16,128,128]{3,2,1,0:T(8,128)S(1)} fusion(f32[128,128,1,1]{1,0,3,2:T(8,128)S(1)} %copy-done.5, f32[4,128,16,128]{3,2,1,0:T(8,128)S(1)} %bitcast.38), kind=kOutput, calls=%fused_computation.4 | convolution fusion | flops 805306368 | bytes 8454144 | tf_op jit(solution)/shard_map/pnyz,nk->pkyz/dot_general | solution.py:32
  113.1 3.5 %fusion.5 = f32[4,128,16,128]{1,3,2,0:T(8,128)} fusion(f32[128,128,1,1]{1,0,3,2:T(8,128)S(1)} %copy-done.4, f32[4,16,128,128]{3,2,1,0:T(8,128)S(1)} %fusion.3, f32[128,16,128]{0,2,1:T(8,128)S(1)} %fusion.7), kind=kOutput, calls=%fused_computation.8 | convolution fusion | flops 806354944 | bytes 9502720 | tf_op jit(solution)/shard_map/pkyz,nk->pnyz/dot_general | solution.py:32
  116.6 5.5 %copy.19 = f32[4,128,16,128]{3,2,0,1:T(8,128)} copy(f32[4,128,16,128]{1,3,2,0:T(8,128)} %fusion.5) | data formatting | bytes 8388608 | tf_op jit(solution)/shard_map/pkyz,nk->pnyz/transpose | solution.py:32
  122.1 5.0 %all-to-all-start.1 = ((f32[4,128,16,128]{3,2,0,1:T(8,128)}), f32[4,128,16,128]{3,2,0,1:T(8,128)}, u32[]{:S(2)}, u32[]{:S(2)}) async-start(f32[4,128,16,128]{3,2,0,1:T(8,128)} %copy.19), calls=%async_computation.1 | async-start | bytes 8388608 | tf_op jit(solution)/shard_map/all_to_all | solution.py:67
  127.1 7.1 %collective-permute-start.1 = (f32[2]{0:T(128)S(1)}, f32[2]{0:T(128)S(1)}, u32[]{:S(2)}, u32[]{:S(2)}) collective-permute-start(f32[2]{0:T(128)S(1)} %get-tuple-element.6), channel_id=1, source_target_pairs={{0,8},{8,16},{16,24},{24,32},{32,40},{40,48},{48,56},{56,64},{64,7... | collective-permute-start | bytes 32 | tf_op jit(solution)/shard_map/ppermute | solution.py:13
  134.2 1.7 broadcast_multiply_fusion.1
  135.9 0.4 broadcast_multiply_fusion.2
  136.3 45.1 %all-to-all-done.1 = f32[4,128,16,128]{3,2,0,1:T(8,128)} async-done(((f32[4,128,16,128]{3,2,0,1:T(8,128)}), f32[4,128,16,128]{3,2,0,1:T(8,128)}, u32[]{:S(2)}, u32[]{:S(2)}) %all-to-all-start.1) | async-done | bytes 4194336 | tf_op jit(solution)/shard_map/all_to_all | solution.py:67
  181.4 2.8 %copy.21 = f32[4,16,8,16,128]{4,3,2,1,0:T(8,128)S(1)} copy(f32[4,16,8,16,128]{4,3,0,1,2:T(8,128)} %bitcast.11) | data formatting | bytes 8388608 | tf_op jit(solution)/shard_map/all_to_all | solution.py:67
  184.2 3.5 %fusion.10 = f32[4,16,128,128]{3,2,1,0:T(8,128)S(1)} fusion(f32[4,16,128,128]{3,2,1,0:T(8,128)S(1)} %bitcast.39, f32[128,128,1,1]{1,0,3,2:T(8,128)S(1)} %copy-done.4), kind=kOutput, calls=%fused_computation.24 | convolution fusion | flops 805306368 | bytes 8454144 | tf_op jit(solution)/shard_map/pxky,nk->pxny/dot_general | solution.py:32
  187.8 3.6 %multiply_reduce_fusion.1 = (f32[2,16,128,128]{3,2,1,0:T(8,128)S(1)}, f32[4,16,128,128]{3,2,1,0:T(8,128)S(1)}) fusion(f32[2,16,128,128]{3,2,1,0:T(8,128)S(1)} %broadcast_multiply_fusion.2, f32[128,128,1,1]{1,0,3,2:T(8,128)S(1)} %copy-done.4, f32[4,16,128,128]{3,2,1,0:T(8,128)S(1)} %fusion.10), kind=kOutput, calls=%fused_computation.7 | convolution fusion | flops 806879232 | bytes 12648448 | tf_op jit(solution)/shard_map/pxyk,nk->pxyn/dot_general | solution.py:32
  191.3 0.9 multiply_reduce_fusion
  192.2 3.4 %collective-permute-start.2 = (f32[2,16,128,128]{3,2,1,0:T(8,128)S(1)}, f32[2,16,128,128]{3,2,1,0:T(8,128)S(1)}, u32[]{:S(2)}, u32[]{:S(2)}) collective-permute-start(f32[2,16,128,128]{3,2,1,0:T(8,128)S(1)} %multiply_reduce_fusion), channel_id=1, source_target_pairs={{0,248},{8,0},{16,8},{24,16},{32,24},{40,32},{48,40},{56,48},{64,5... | collective-permute-start | bytes 6291464 | tf_op jit(solution)/shard_map/ppermute | solution.py:13
  195.7 33.8 %collective-permute-done.2 = f32[2,16,128,128]{3,2,1,0:T(8,128)S(1)} collective-permute-done((f32[2,16,128,128]{3,2,1,0:T(8,128)S(1)}, f32[2,16,128,128]{3,2,1,0:T(8,128)S(1)}, u32[]{:S(2)}, u32[]{:S(2)}) %collective-permute-start.2) | collective-permute-done | bytes 2097184 | tf_op jit(solution)/shard_map/ppermute | solution.py:13
  229.5 1.6 add.48
  (24 shorter events, 0.5 us)
Async XLA Ops:
  0.0 28.4 %copy-start.4 = (f32[128,128,1,1]{1,0,3,2:T(8,128)S(1)}, f32[128,128,1,1]{1,0,3,2:T(8,128)}, u32[]{:S(2)}) copy-start(f32[128,128,1,1]{1,0,3,2:T(8,128)} %constant.35) | copy-start | bytes 196612
  0.0 25.5 %collective-permute-start = (f32[2,16,128,128]{3,2,1,0:T(8,128)}, f32[2,16,128,128]{3,2,1,0:T(8,128)S(1)}, u32[]{:S(2)}, u32[]{:S(2)}) collective-permute-start(f32[2,16,128,128]{3,2,1,0:T(8,128)} %param.11), channel_id=1, source_target_pairs={{0,8},{8,16},{16,24},{24,32},{32,40},{40,48},{48,56},{56,64},{64,7... | collective-permute-start | bytes 6291464 | tf_op jit(solution)/shard_map/ppermute | solution.py:13
  25.5 2.9 %copy-start.1 = (f32[2,16,128,128]{3,2,1,0:T(8,128)}, f32[2,16,128,128]{3,2,1,0:T(8,128)S(1)}, u32[]{:S(2)}) copy-start(f32[2,16,128,128]{3,2,1,0:T(8,128)S(1)} %collective-permute-done) | copy-start | bytes 6291460
  39.2 5.4 %copy-start.8 = (f32[128]{0:T(128)S(1)}, f32[128]{0:T(128)}, u32[]{:S(2)}) copy-start(f32[128]{0:T(128)} %constant.28.clone) | copy-start | bytes 1540
  39.2 5.4 %copy-start.6 = (f32[128]{0:T(128)S(1)}, f32[128]{0:T(128)}, u32[]{:S(2)}) copy-start(f32[128]{0:T(128)} %constant.34) | copy-start | bytes 1540
  39.2 65.4 %all-to-all-start = ((f32[4,16,128,128]{3,1,0,2:T(8,128)}), f32[4,16,128,128]{3,1,0,2:T(8,128)}, u32[]{:S(2)}, u32[]{:S(2)}) async-start(f32[4,16,128,128]{3,1,0,2:T(8,128)} %copy.16), calls=%async_computation | async-start | bytes 8388608 | tf_op jit(solution)/shard_map/all_to_all | solution.py:64
  45.0 64.2 %copy-start.5 = (f32[128,128,1,1]{1,0,3,2:T(8,128)S(1)}, f32[128,128,1,1]{1,0,3,2:T(8,128)}, u32[]{:S(2)}) copy-start(f32[128,128,1,1]{1,0,3,2:T(8,128)} %constant.36) | copy-start | bytes 196612
  122.1 5.0 %copy-start.7 = (s32[2]{0:T(128)S(1)}, s32[2]{0:T(128)}, u32[]{:S(2)}) copy-start(s32[2]{0:T(128)} %param.12) | copy-start | bytes 28
  122.1 12.1 %copy-start = (f32[2,16,128,128]{3,2,1,0:T(8,128)S(1)}, f32[2,16,128,128]{3,2,1,0:T(8,128)}, u32[]{:S(2)}) copy-start(f32[2,16,128,128]{3,2,1,0:T(8,128)} %param.11) | copy-start | bytes 6291460
  122.1 59.3 %all-to-all-start.1 = ((f32[4,128,16,128]{3,2,0,1:T(8,128)}), f32[4,128,16,128]{3,2,0,1:T(8,128)}, u32[]{:S(2)}, u32[]{:S(2)}) async-start(f32[4,128,16,128]{3,2,0,1:T(8,128)} %copy.19), calls=%async_computation.1 | async-start | bytes 8388608 | tf_op jit(solution)/shard_map/all_to_all | solution.py:67
  127.1 8.8 %copy-start.2 = (f32[2,16,128,128]{3,2,1,0:T(8,128)S(1)}, f32[2,16,128,128]{3,2,1,0:T(8,128)}, u32[]{:S(2)}) copy-start(f32[2,16,128,128]{3,2,1,0:T(8,128)} %copy-done.1) | copy-start | bytes 6291460
  127.1 8.8 %collective-permute-start.1 = (f32[2]{0:T(128)S(1)}, f32[2]{0:T(128)S(1)}, u32[]{:S(2)}, u32[]{:S(2)}) collective-permute-start(f32[2]{0:T(128)S(1)} %get-tuple-element.6), channel_id=1, source_target_pairs={{0,8},{8,16},{16,24},{24,32},{32,40},{40,48},{48,56},{56,64},{64,7... | collective-permute-start | bytes 32 | tf_op jit(solution)/shard_map/ppermute | solution.py:13
  187.7 3.6 %copy-start.3 = (f32[2,16,128,128]{3,2,1,0:T(8,128)S(1)}, f32[2,16,128,128]{3,2,1,0:T(8,128)}, u32[]{:S(2)}) copy-start(f32[2,16,128,128]{3,2,1,0:T(8,128)} %broadcast_multiply_fusion.1) | copy-start | bytes 6291460
  192.2 37.3 %collective-permute-start.2 = (f32[2,16,128,128]{3,2,1,0:T(8,128)S(1)}, f32[2,16,128,128]{3,2,1,0:T(8,128)S(1)}, u32[]{:S(2)}, u32[]{:S(2)}) collective-permute-start(f32[2,16,128,128]{3,2,1,0:T(8,128)S(1)} %multiply_reduce_fusion), channel_id=1, source_target_pairs={{0,248},{8,0},{16,8},{24,16},{32,24},{40,32},{48,40},{56,48},{64,5... | collective-permute-start | bytes 6291464 | tf_op jit(solution)/shard_map/ppermute | solution.py:13
where the time goes:
time: 232 us; the launch traced here: 231 us
  waiting for transfers between devices  162 us (70%)
  starting transfers between devices  23.1 us (10%)
  matrix products  19.7 us (8%)
  local copies, waits for them, and re-layouts  18.5 us (8%)
  other arithmetic  7.77 us (3%)
    all_to_all x1, waiting for transfers between devices, shards(): field = lax.all_to_all(field, 'pw', split_axis=2, concat_axis=1, tiled=True)  59.6 us
    ppermute x3, waiting for transfers between devices, passed_along(): return lax.ppermute(value, axis, pairs)  57.1 us
    all_to_all x1, waiting for transfers between devices, shards(): field = lax.all_to_all(field, 'pw', split_axis=1, concat_axis=2, tiled=True)  45.1 us
    dot_general x6, matrix products, apply_table(): return jnp.einsum(form, field, table, precision=lax.Precision.HIGH)  19.7 us
    ppermute x3, starting transfers between devices, passed_along(): return lax.ppermute(value, axis, pairs)  12.8 us
    transpose x2, local copies, waits for them, and re-layouts, apply_table(): return jnp.einsum(form, field, table, precision=lax.Precision.HIGH)  11 us
    all_to_all x1, starting transfers between devices, shards(): field = lax.all_to_all(field, 'pw', split_axis=2, concat_axis=1, tiled=True)  5.36 us
    all_to_all x1, starting transfers between devices, shards(): field = lax.all_to_all(field, 'pw', split_axis=1, concat_axis=2, tiled=True)  4.98 us
  transfers between devices with their start and end apart: 5, of which 4 were waited for; matrix products, arithmetic and copies ran while one was open for 1% of the time, Pallas kernels for 0%

commit v1 on v0

v1 whole, which is shorter than its diff:
```python
import functools

import jax
import jax.numpy as jnp
import numpy as np
from jax import lax
from jax.experimental import pallas as pl
from jax.experimental.pallas import tpu as pltpu
from jax.sharding import PartitionSpec as P

MIXING = 0.25
N = 128
HALF = N // 2
SLAB = 16
HALVES = 2
ROWS = SLAB // HALVES
MESH = pl.DeviceIdType.MESH
FAR_FIRST = ((2, 1), (2, 0), (1, 1), (3, 1), (0, 1), (1, 0), (3, 0))
PAIRS = ((0, 0), (1, 0), (0, 1), (1, 1))


def tables():
    grid = np.arange(N)
    cosines = [np.cos(2.0 * np.pi * (k * grid % N) / N) for k in range(HALF + 1)]
    sines = [np.sin(2.0 * np.pi * (k * grid % N) / N) for k in range(1, HALF)]
    table = np.stack(cosines + sines, axis=1).astype(np.float32)
    high = table.astype(jnp.bfloat16)
    low = (table - high.astype(np.float32)).astype(jnp.bfloat16)
    right_forward = np.block([[high, low], [high, low]])
    left_forward = np.block([[high.T, high.T], [low.T, low.T]])
    left_inverse = np.block([[high, high], [low, low]])
    right_inverse = np.block([[high.T, low.T], [high.T, low.T]])
    return np.stack([right_forward, left_forward, left_inverse, right_inverse])


def split(value):
    high = value.astype(jnp.bfloat16)
    low = (value - high.astype(jnp.float32)).astype(jnp.bfloat16)
    return high, low


def from_right(value, table):
    high, low = split(value)
    both = jnp.dot(
        jnp.concatenate([high, low], axis=1), table, preferred_element_type=jnp.float32
    )
    return both[:, :N] + both[:, N:]


def from_left(table, value):
    high, low = split(value)
    both = jnp.dot(
        table, jnp.concatenate([high, low], axis=0), preferred_element_type=jnp.float32
    )
    return both[:N] + both[N:]


def side_by_side(value):
    return jnp.concatenate([value[:N], value[N:]], axis=1)


def stacked(value):
    return jnp.concatenate([value[:, :N], value[:, N:]], axis=0)


def wave_numbers(index):
    wave = jnp.where(index > HALF, index - HALF, index)
    share = jnp.where((wave == 0) | (wave == HALF), 1.0 / N, 2.0 / N)
    wave = wave.astype(jnp.float32) * (2.0 * np.pi / N)
    return wave * wave, share


def kernel(
    occupations, orbitals, table, out, passing, weights, passed_weights, sent, middle, back,
    theirs, returned, coulomb, turned, pass_send, pass_recv, weight_send, weight_recv, go_send,
    go_recv, come_send, come_recv, term_send, term_recv, local_sem,
):
    band = lax.axis_index("band")
    place = lax.axis_index("pw")
    bands = lax.axis_size("band")
    following = {"band": lax.rem(band + 1, bands)}
    previous = {"band": lax.rem(band + bands - 1, bands)}
    place_x, place_y = lax.rem(place, 4), lax.div(place, 4)
    peers = [
        lax.rem(place_y + dy, 2) * 4 + lax.rem(place_x + dx, 4) for dx, dy in FAR_FIRST
    ]

    for i in range(2):
        weight = occupations[i].astype(jnp.float32) * (-0.5 * MIXING)
        weights[i] = jnp.full((8, N), weight, jnp.float32)

    barrier = pltpu.get_barrier_semaphore()
    for device in [following, previous] + [{"pw": peer} for peer in peers]:
        pl.semaphore_signal(barrier, inc=1, device_id=device, device_id_type=MESH)
    pl.semaphore_wait(barrier, 2 + len(peers))

    passes = [
        pltpu.make_async_remote_copy(
            src_ref=orbitals.at[j], dst_ref=passing.at[j], send_sem=pass_send.at[j],
            recv_sem=pass_recv.at[j], device_id=following, device_id_type=MESH,
        )
        for j in range(2)
    ]
    weight_pass = pltpu.make_async_remote_copy(
        src_ref=weights, dst_ref=passed_weights, send_sem=weight_send, recv_sem=weight_recv,
        device_id=following, device_id_type=MESH,
    )
    passes[0].start()
    weight_pass.start()
    passes[1].start()

    def slab(index):
        return pl.ds(pl.multiple_of(index * SLAB, SLAB), SLAB)

    goes, comes, stays = [], [], []
    for p in range(4):
        goes.append([
            pltpu.make_async_remote_copy(
                src_ref=sent.at[p, slab(peer)], dst_ref=middle.at[p, :, slab(place)],
                send_sem=go_send.at[p, n], recv_sem=go_recv.at[p, n],
                device_id={"pw": peer}, device_id_type=MESH,
            )
            for n, peer in enumerate(peers)
        ])
        comes.append([
            pltpu.make_async_remote_copy(
                src_ref=middle.at[p, :, slab(peer)], dst_ref=back.at[p, slab(place)],
                send_sem=come_send.at[p, n], recv_sem=come_recv.at[p, n],
                device_id={"pw": peer}, device_id_type=MESH,
            )
            for n, peer in enumerate(peers)
        ])
        stays.append((
            pltpu.make_async_copy(
                sent.at[p, slab(place)], middle.at[p, :, slab(place)], local_sem.at[p, 0]
            ),
            pltpu.make_async_copy(
                middle.at[p, :, slab(place)], back.at[p, slab(place)], local_sem.at[p, 1]
            ),
        ))
    terms = [
        [
            pltpu.make_async_remote_copy(
                src_ref=theirs.at[j, pl.ds(h * ROWS, ROWS)],
                dst_ref=returned.at[j, pl.ds(h * ROWS, ROWS)],
                send_sem=term_send.at[j, h], recv_sem=term_recv.at[j, h],
                device_id=previous, device_id_type=MESH,
            )
            for h in range(HALVES)
        ]
        for j in range(2)
    ]

    for p, (i, j) in enumerate(PAIRS):
        if i == 0:
            passes[j].wait_recv()

        @pl.loop(0, HALVES)
        def _(h):
            @pl.loop(0, ROWS // 4)
            def _(quad):
                for r in range(2):
                    at = pl.ds(h * ROWS + quad * 4 + r * 2, 2)
                    field = (orbitals[i, at] * passing[j, at]).reshape(2 * N, N)
                    field = from_right(field, table[0])
                    field = from_left(table[1], side_by_side(field))
                    turned[quad * 4 + r * 2] = field[:, :N]
                    turned[quad * 4 + r * 2 + 1] = field[:, N:]

            @pl.loop(0, N // 16)
            def _(block):
                for b in range(2):
                    rows = pl.ds(pl.multiple_of(block * 16 + b * 8, 8), 8)
                    sent[p, rows, pl.ds(pl.multiple_of(h * ROWS, ROWS), ROWS)] = jnp.swapaxes(
                        turned[:, rows], 0, 1
                    )

        stays[p][0].start()
        for copy in goes[p]:
            copy.start()
        if p == 1:
            wave_x, share_x = wave_numbers(lax.broadcasted_iota(jnp.int32, (N, N), 0))
            wave_z, share_z = wave_numbers(lax.broadcasted_iota(jnp.int32, (N, N), 1))
            square_xz = wave_x + wave_z
            share_xz = share_x * share_z

            @pl.loop(0, SLAB)
            def _(y):
                wave_y, share_y = wave_numbers(
                    jnp.full((N, N), place * SLAB + y, jnp.int32)
                )
                square = square_xz + wave_y
                safe = jnp.where(square > 0, square, 1.0)
                factor = (4.0 * np.pi) * (share_xz * share_y)
                coulomb[y] = jnp.where(square > 0, factor / safe, 0.0)

    for p in range(4):
        stays[p][0].wait()
        for copy in goes[p]:
            copy.wait_recv()

        @pl.loop(0, SLAB // 4)
        def _(quad):
            for r in range(2):
                y = quad * 4 + r * 2
                field = jnp.concatenate([middle[p, y], middle[p, y + 1]], axis=1)
                field = from_left(table[1], field)
                field = field * jnp.concatenate([coulomb[y], coulomb[y + 1]], axis=1)
                field = from_left(table[2], field)
                middle[p, y] = field[:, :N]
                middle[p, y + 1] = field[:, N:]

        stays[p][1].start()
        for copy in comes[p]:
            copy.start()

    weight_pass.wait_recv()
    for p, (i, j) in enumerate(PAIRS):
        stays[p][1].wait()
        for copy in comes[p]:
            copy.wait_recv()
        for h in range(HALVES):

            @pl.loop(0, N // 16)
            def _(block):
                for b in range(2):
                    rows = pl.ds(pl.multiple_of(block * 16 + b * 8, 8), 8)
                    turned[:, rows] = jnp.swapaxes(back[p, rows, h * ROWS : (h + 1) * ROWS], 0, 1)

            @pl.loop(0, ROWS // 4)
            def _(quad):
                for r in range(2):
                    y = quad * 4 + r * 2
                    field = jnp.concatenate([turned[y], turned[y + 1]], axis=1)
                    field = from_left(table[2], field)
                    field = from_right(stacked(field), table[3])
                    potential = field.reshape(2, N // 8, 8, N)
                    at = pl.ds(h * ROWS + y, 2)
                    mine = (
                        potential * passing[j, at].reshape(2, N // 8, 8, N) * passed_weights[j]
                    ).reshape(2, N, N)
                    other = (
                        potential * orbitals[i, at].reshape(2, N // 8, 8, N) * weights[i]
                    ).reshape(2, N, N)
                    if j == 0:
                        out[i, at] = mine
                    else:
                        out[i, at] += mine
                    if i == 0:
                        theirs[j, at] = other
                    else:
                        theirs[j, at] += other

            if i == 1:
                terms[j][h].start()

    for j in range(2):
        for h in range(HALVES):
            terms[j][h].wait_recv()

            @pl.loop(0, ROWS)
            def _(row):
                out[j, h * ROWS + row] += returned[j, h * ROWS + row]

    for copy in passes + [weight_pass]:
        copy.wait_send()
    for p in range(4):
        for copy in goes[p] + comes[p]:
            copy.wait_send()
    for j in range(2):
        for h in range(HALVES):
            terms[j][h].wait_send()


def shards(orbitals, occupations):
    vmem = pl.BlockSpec(memory_space=pltpu.VMEM)
    dma = pltpu.SemaphoreType.DMA
    field = (N, SLAB, N)
    return pl.pallas_call(
        kernel,
        out_shape=jax.ShapeDtypeStruct(orbitals.shape, jnp.float32),
        in_specs=[pl.BlockSpec(memory_space=pltpu.SMEM), vmem, vmem],
        out_specs=vmem,
        scratch_shapes=[
            pltpu.VMEM(orbitals.shape, jnp.float32),
            pltpu.VMEM((2, 8, N), jnp.float32),
            pltpu.VMEM((2, 8, N), jnp.float32),
            pltpu.VMEM((4, N, SLAB, N), jnp.float32),
            pltpu.VMEM((4, SLAB, N, N), jnp.float32),
            pltpu.VMEM((4, N, SLAB, N), jnp.float32),
            pltpu.VMEM(orbitals.shape, jnp.float32),
            pltpu.VMEM(orbitals.shape, jnp.float32),
            pltpu.VMEM((SLAB, N, N), jnp.float32),
            pltpu.VMEM((ROWS, N, N), jnp.float32),
            dma((2,)), dma((2,)), dma, dma,
            dma((4, 7)), dma((4, 7)), dma((4, 7)), dma((4, 7)),
            dma((2, HALVES)), dma((2, HALVES)), dma((4, 2)),
        ],
        compiler_params=pltpu.CompilerParams(
            collective_id=0, has_side_effects=True, vmem_limit_bytes=48 * 1024 * 1024
        ),
        name="exchange",
    )(occupations, orbitals, jnp.asarray(tables()))


def solution(mesh):
    placed = (P("band", "pw", None, None), P("band"))
    return jax.shard_map(
        shards, mesh=mesh, in_specs=placed, out_specs=P("band", "pw", None, None), check_vma=False
    )
```

time: 232 us -> 148 us (0.64)
  the two profiles are of different devices: /device:TPU:71 before, /device:TPU:8 now
where the time goes in v1:
time: 148 us
  Pallas kernels  143 us (97%)
  local copies, waits for them, and re-layouts  4.61 us (3%)
    pallas_call x1, Pallas kernels, shards(): pl.pallas_call(kernel, out_shape=jax.ShapeDtypeStruct(orbitals.shape, jnp...  143 us
    unnamed x7, local copies, waits for them, and re-layouts  4.61 us

profile of v1, /device:TPU:8, one launch (start us, length us, event | category | flops | bytes accessed | tf_op | source)
XLA Modules:
  0.0 148.1 jit_solution(15788911265348232366)
XLA Ops:
  0.0 0.0 copy-start
  0.0 1.6 %copy-done = f32[2,16,128,128]{3,2,1,0:T(8,128)S(1)} copy-done((f32[2,16,128,128]{3,2,1,0:T(8,128)S(1)}, f32[2,16,128,128]{3,2,1,0:T(8,128)}, u32[]{:S(2)}) %copy-start) | copy-done | bytes 2097176
  1.6 0.0 copy-start.1
  1.6 1.0 copy-done.1
  2.6 0.0 copy-start.2
  2.6 0.7 copy-done.2
  3.3 143.5 %exchange.1 = f32[2,16,128,128]{3,2,1,0:T(8,128)S(1)} custom-call(s32[2]{0:T(128)S(1)} %copy-done.2, f32[2,16,128,128]{3,2,1,0:T(8,128)S(1)} %copy-done, bf16[4,256,256]{2,1,0:T(8,128)(2,1)S(1)} %copy-done.1), custom_call_target="tpu_custom_call" | custom-call | tf_op jit(solution)/shard_map/exchange/pallas_call | solution.py:279
  146.8 1.3 copy.5
Async XLA Ops:
  0.0 1.6 %copy-start = (f32[2,16,128,128]{3,2,1,0:T(8,128)S(1)}, f32[2,16,128,128]{3,2,1,0:T(8,128)}, u32[]{:S(2)}) copy-start(f32[2,16,128,128]{3,2,1,0:T(8,128)} %orbitals.1) | copy-start | bytes 6291460
  1.6 1.0 copy-start.1
  2.6 0.7 copy-start.2

commit v2 on v1

--- a/solution.py
+++ b/solution.py
@@ -17,6 +17,8 @@
 MESH = pl.DeviceIdType.MESH
 FAR_FIRST = ((2, 1), (2, 0), (1, 1), (3, 1), (0, 1), (1, 0), (3, 0))
 PAIRS = ((0, 0), (1, 0), (0, 1), (1, 1))
+PARTS = 4
+PART = SLAB // PARTS
 
 
 def tables():
@@ -72,42 +74,136 @@
 
 def kernel(
     occupations, orbitals, table, out, passing, weights, passed_weights, sent, middle, back,
-    theirs, returned, coulomb, turned, pass_send, pass_recv, weight_send, weight_recv, go_send,
-    go_recv, come_send, come_recv, term_send, term_recv, local_sem,
+    theirs, returned, coulomb, turned, pass_relay, term_relay, pass_send, pass_recv, weight_send,
+    weight_recv, go_send, go_recv, come_send, come_recv, term_send, term_recv, local_sem,
+    relay_send, relay_recv,
 ):
     band = lax.axis_index("band")
     place = lax.axis_index("pw")
     bands = lax.axis_size("band")
+    ring = bands // 2
+    spot, base = lax.rem(band, ring), (band // ring) * ring
+    across = lax.rem(base + ring, bands)
     following = {"band": lax.rem(band + 1, bands)}
     previous = {"band": lax.rem(band + bands - 1, bands)}
     place_x, place_y = lax.rem(place, 4), lax.div(place, 4)
     peers = [
         lax.rem(place_y + dy, 2) * 4 + lax.rem(place_x + dx, 4) for dx, dy in FAR_FIRST
     ]
+    is_first, is_last = spot == 0, spot == ring - 1
+    is_second, is_second_last = spot == 2, spot == ring - 3
+    first, last, second, second_last = 0, ring - 1, 2, ring - 3
+    pass_relays = (None, last, second, second_last)
+    term_relays = (None, first, second_last, second)
 
     for i in range(2):
         weight = occupations[i].astype(jnp.float32) * (-0.5 * MIXING)
         weights[i] = jnp.full((8, N), weight, jnp.float32)
 
     barrier = pltpu.get_barrier_semaphore()
+
+    def greet(device):
+        pl.semaphore_signal(barrier, inc=1, device_id=device, device_id_type=MESH)
+
     for device in [following, previous] + [{"pw": peer} for peer in peers]:
-        pl.semaphore_signal(barrier, inc=1, device_id=device, device_id_type=MESH)
-    pl.semaphore_wait(barrier, 2 + len(peers))
-
-    passes = [
-        pltpu.make_async_remote_copy(
-            src_ref=orbitals.at[j], dst_ref=passing.at[j], send_sem=pass_send.at[j],
-            recv_sem=pass_recv.at[j], device_id=following, device_id_type=MESH,
-        )
-        for j in range(2)
-    ]
+        greet(device)
+    for here, others in (
+        (is_first, ((first, 0), (last, 1), (second, 2), (second_last, 2))),
+        (is_last, ((last, 0), (first, 1), (second, 2), (second_last, 2))),
+        (is_second, ((first, 2), (last, 2))),
+        (is_second_last, ((first, 2), (last, 2))),
+    ):
+
+        @pl.when(here)
+        def _():
+            for other, side in others:
+                if side != 0:
+                    greet({"band": base + other})
+                if side != 1:
+                    greet({"band": across + other})
+
+    at_end = (is_first | is_last).astype(jnp.int32)
+    beside = (is_second | is_second_last).astype(jnp.int32)
+    pl.semaphore_wait(barrier, 2 + len(peers) + 6 * at_end + 4 * beside)
+
+    def part(q):
+        return pl.ds(q * PART, PART)
+
+    def routes(source, target, relay, sends, recvs, relay_sends, relay_recvs, onward, relays, end):
+        direct, there, then = [], [], []
+        for j in range(2):
+            for q in range(PARTS):
+                direct.append(pltpu.make_async_remote_copy(
+                    src_ref=source.at[j, part(q)], dst_ref=target.at[j, part(q)],
+                    send_sem=sends.at[j, q], recv_sem=recvs.at[j, q],
+                    device_id=onward, device_id_type=MESH,
+                ))
+                if relays[q] is None:
+                    there.append(None)
+                    then.append(None)
+                    continue
+                there.append(pltpu.make_async_remote_copy(
+                    src_ref=source.at[j, part(q)], dst_ref=relay.at[j],
+                    send_sem=sends.at[j, q], recv_sem=relay_recvs.at[j],
+                    device_id={"band": across + relays[q]}, device_id_type=MESH,
+                ))
+                then.append(pltpu.make_async_remote_copy(
+                    src_ref=relay.at[j], dst_ref=target.at[j, part(q)],
+                    send_sem=relay_sends.at[j], recv_sem=recvs.at[j, q],
+                    device_id={"band": base + end}, device_id_type=MESH,
+                ))
+        return direct, there, then
+
+    pass_direct, pass_there, pass_then = routes(
+        orbitals, passing, pass_relay, pass_send, pass_recv, relay_send.at[0], relay_recv.at[0],
+        following, pass_relays, first,
+    )
+    term_direct, term_there, term_then = routes(
+        theirs, returned, term_relay, term_send, term_recv, relay_send.at[1], relay_recv.at[1],
+        previous, term_relays, last,
+    )
+
+    def start(direct, there, is_end, j, q):
+        n = j * PARTS + q
+        if there[n] is None:
+            direct[n].start()
+            return
+
+        @pl.when(is_end)
+        def _():
+            there[n].start()
+
+        @pl.when(jnp.logical_not(is_end))
+        def _():
+            direct[n].start()
+
+    roles = {first: is_first, last: is_last, second: is_second, second_last: is_second_last}
+
+    def relay_on(there, then, relays, j):
+        for q in range(1, PARTS):
+            n = j * PARTS + q
+
+            @pl.when(roles[relays[q]])
+            def _():
+                there[n].wait_recv()
+                then[n].start()
+
+    def relay_end(then, relays):
+        for q in range(1, PARTS):
+
+            @pl.when(roles[relays[q]])
+            def _():
+                for j in range(2):
+                    then[j * PARTS + q].wait_send()
+
     weight_pass = pltpu.make_async_remote_copy(
         src_ref=weights, dst_ref=passed_weights, send_sem=weight_send, recv_sem=weight_recv,
         device_id=following, device_id_type=MESH,
     )
-    passes[0].start()
+    for j in range(2):
+        for q in range(PARTS):
+            start(pass_direct, pass_there, is_last, j, q)
     weight_pass.start()
-    passes[1].start()
 
     def slab(index):
         return pl.ds(pl.multiple_of(index * SLAB, SLAB), SLAB)
@@ -138,22 +234,11 @@
                 middle.at[p, :, slab(place)], back.at[p, slab(place)], local_sem.at[p, 1]
             ),
         ))
-    terms = [
-        [
-            pltpu.make_async_remote_copy(
-                src_ref=theirs.at[j, pl.ds(h * ROWS, ROWS)],
-                dst_ref=returned.at[j, pl.ds(h * ROWS, ROWS)],
-                send_sem=term_send.at[j, h], recv_sem=term_recv.at[j, h],
-                device_id=previous, device_id_type=MESH,
-            )
-            for h in range(HALVES)
-        ]
-        for j in range(2)
-    ]
-
     for p, (i, j) in enumerate(PAIRS):
         if i == 0:
-            passes[j].wait_recv()
+            relay_on(pass_there, pass_then, pass_relays, j)
+            for q in range(PARTS):
+                pass_direct[j * PARTS + q].wait_recv()
 
         @pl.loop(0, HALVES)
         def _(h):
@@ -252,24 +337,27 @@
                         theirs[j, at] += other
 
             if i == 1:
-                terms[j][h].start()
+                for q in range(h * PARTS // HALVES, (h + 1) * PARTS // HALVES):
+                    start(term_direct, term_there, is_first, j, q)
 
     for j in range(2):
-        for h in range(HALVES):
-            terms[j][h].wait_recv()
-
-            @pl.loop(0, ROWS)
+        relay_on(term_there, term_then, term_relays, j)
+    for j in range(2):
+        for q in range(PARTS):
+            term_direct[j * PARTS + q].wait_recv()
+
+            @pl.loop(0, PART)
             def _(row):
-                out[j, h * ROWS + row] += returned[j, h * ROWS + row]
-
-    for copy in passes + [weight_pass]:
+                out[j, q * PART + row] += returned[j, q * PART + row]
+
+    relay_end(pass_then, pass_relays)
+    relay_end(term_then, term_relays)
+    weight_pass.wait_send()
+    for copy in pass_direct + term_direct:
         copy.wait_send()
     for p in range(4):
         for copy in goes[p] + comes[p]:
             copy.wait_send()
-    for j in range(2):
-        for h in range(HALVES):
-            terms[j][h].wait_send()
 
 
 def shards(orbitals, occupations):
@@ -292,9 +380,11 @@
             pltpu.VMEM(orbitals.shape, jnp.float32),
             pltpu.VMEM((SLAB, N, N), jnp.float32),
             pltpu.VMEM((ROWS, N, N), jnp.float32),
-            dma((2,)), dma((2,)), dma, dma,
+            pltpu.VMEM((2, PART, N, N), jnp.float32),
+            pltpu.VMEM((2, PART, N, N), jnp.float32),
+            dma((2, PARTS)), dma((2, PARTS)), dma, dma,
             dma((4, 7)), dma((4, 7)), dma((4, 7)), dma((4, 7)),
-            dma((2, HALVES)), dma((2, HALVES)), dma((4, 2)),
+            dma((2, PARTS)), dma((2, PARTS)), dma((4, 2)), dma((2, 2)), dma((2, 2)),
         ],
         compiler_params=pltpu.CompilerParams(
             collective_id=0, has_side_effects=True, vmem_limit_bytes=48 * 1024 * 1024

time: 148 us -> 137 us (0.926)
  the two profiles are of different devices: /device:TPU:8 before, /device:TPU:1 now
where the time goes in v2:
time: 137 us; the launch traced here: 135 us
  Pallas kernels  130 us (95%)
  local copies, waits for them, and re-layouts  4.61 us (3%)
    pallas_call x1, Pallas kernels, shards(): pl.pallas_call(kernel, out_shape=jax.ShapeDtypeStruct(orbitals.shape, jnp...  130 us
    unnamed x7, local copies, waits for them, and re-layouts  4.61 us

profile of v2, /device:TPU:1, one launch (start us, length us, event | category | flops | bytes accessed | tf_op | source)
XLA Modules:
  0.0 134.6 jit_solution(18183661790977559055)
XLA Ops:
  0.0 0.0 copy-start
  0.0 1.6 %copy-done = f32[2,16,128,128]{3,2,1,0:T(8,128)S(1)} copy-done((f32[2,16,128,128]{3,2,1,0:T(8,128)S(1)}, f32[2,16,128,128]{3,2,1,0:T(8,128)}, u32[]{:S(2)}) %copy-start) | copy-done | bytes 2097176
  1.6 0.0 copy-start.1
  1.6 1.0 copy-done.1
  2.6 0.0 copy-start.2
  2.6 0.7 copy-done.2
  3.3 129.9 %exchange.1 = f32[2,16,128,128]{3,2,1,0:T(8,128)S(1)} custom-call(s32[2]{0:T(128)S(1)} %copy-done.2, f32[2,16,128,128]{3,2,1,0:T(8,128)S(1)} %copy-done, bf16[4,256,256]{2,1,0:T(8,128)(2,1)S(1)} %copy-done.1), custom_call_target="tpu_custom_call" | custom-call | tf_op jit(solution)/shard_map/exchange/pallas_call | solution.py:367
  133.2 1.3 copy.5
Async XLA Ops:
  0.0 1.6 %copy-start = (f32[2,16,128,128]{3,2,1,0:T(8,128)S(1)}, f32[2,16,128,128]{3,2,1,0:T(8,128)}, u32[]{:S(2)}) copy-start(f32[2,16,128,128]{3,2,1,0:T(8,128)} %orbitals.1) | copy-start | bytes 6291460
  1.6 1.0 copy-start.1
  2.6 0.7 copy-start.2

commit v3 on v1

v3 whole, which is shorter than its diff:
```python
import functools

import jax
import jax.numpy as jnp
import numpy as np
from jax import lax
from jax.experimental import pallas as pl
from jax.experimental.pallas import tpu as pltpu
from jax.sharding import PartitionSpec as P

MIXING = 0.25
N = 128
HALF = N // 2
SLAB = 16
HALVES = 2
ROWS = SLAB // HALVES
MESH = pl.DeviceIdType.MESH
FAR_FIRST = ((2, 1), (2, 0), (1, 1), (3, 1), (0, 1), (1, 0), (3, 0))
PARTS = 8
TURNS = ((0, 0), (0, 1), (0, 2), (0, 3))
PART = SLAB // PARTS


def tables():
    grid = np.arange(N)
    cosines = [np.cos(2.0 * np.pi * (k * grid % N) / N) for k in range(HALF + 1)]
    sines = [np.sin(2.0 * np.pi * (k * grid % N) / N) for k in range(1, HALF)]
    table = np.stack(cosines + sines, axis=1).astype(np.float32)
    high = table.astype(jnp.bfloat16)
    low = (table - high.astype(np.float32)).astype(jnp.bfloat16)
    right_forward = np.block([[high, low], [high, low]])
    left_forward = np.block([[high.T, high.T], [low.T, low.T]])
    left_inverse = np.block([[high, high], [low, low]])
    right_inverse = np.block([[high.T, low.T], [high.T, low.T]])
    return np.stack([right_forward, left_forward, left_inverse, right_inverse])


def split(value):
    high = value.astype(jnp.bfloat16)
    low = (value - high.astype(jnp.float32)).astype(jnp.bfloat16)
    return high, low


def from_right(value, table):
    high, low = split(value)
    both = jnp.dot(
        jnp.concatenate([high, low], axis=1), table, preferred_element_type=jnp.float32
    )
    return both[:, :N] + both[:, N:]


def from_left(table, value):
    high, low = split(value)
    both = jnp.dot(
        table, jnp.concatenate([high, low], axis=0), preferred_element_type=jnp.float32
    )
    return both[:N] + both[N:]


def side_by_side(value):
    return jnp.concatenate([value[:N], value[N:]], axis=1)


def stacked(value):
    return jnp.concatenate([value[:, :N], value[:, N:]], axis=0)


def wave_numbers(index):
    wave = jnp.where(index > HALF, index - HALF, index)
    share = jnp.where((wave == 0) | (wave == HALF), 1.0 / N, 2.0 / N)
    wave = wave.astype(jnp.float32) * (2.0 * np.pi / N)
    return wave * wave, share


def kernel(
    occupations_in, orbitals_in, table_in, out, occupations, orbitals, table, passing, weights,
    passed_weights, sent, middle, back, theirs, returned, coulomb, turned, pass_relay, term_relay,
    input_sem, pass_send, pass_recv, weight_send, weight_recv, go_send, go_recv, come_send,
    come_recv, term_send, term_recv, relay_send, relay_recv, turn,
):
    inputs = [
        pltpu.make_async_copy(orbitals_in, orbitals, input_sem.at[0]),
        pltpu.make_async_copy(table_in, table, input_sem.at[1]),
        pltpu.make_async_copy(occupations_in, occupations, input_sem.at[2]),
    ]
    for copy in inputs:
        copy.start()
    band = lax.axis_index("band")
    place = lax.axis_index("pw")
    bands = lax.axis_size("band")
    ring = bands // 2
    spot, base = lax.rem(band, ring), (band // ring) * ring
    across = lax.rem(base + ring, bands)
    following = {"band": lax.rem(band + 1, bands)}
    previous = {"band": lax.rem(band + bands - 1, bands)}
    place_x, place_y = lax.rem(place, 4), lax.div(place, 4)
    peers = [
        lax.rem(place_y + dy, 2) * 4 + lax.rem(place_x + dx, 4) for dx, dy in FAR_FIRST
    ]
    first, last = 0, ring - 1
    near_pass, near_term = (None, last) * 4, (None, first + 1) * 4
    far_pass = (3, ring - 3, 5, ring - 5) * 2
    far_term = (ring - 3, ring - 5, ring - 7, ring - 5)
    pass_routes = {(j, q): (near_pass, far_pass)[j][q] for j in range(2) for q in range(PARTS)}
    term_routes = {
        (j, q): (far_term + near_term)[q] for j in range(2) for q in range(PARTS)
    }
    pass_relays = sorted({relay for relay in pass_routes.values() if relay is not None})
    term_relays = sorted({relay for relay in term_routes.values() if relay is not None})

    greetings = {}
    for here, there, far in (
        [(last, relay, True) for relay in pass_relays]
        + [(first, relay, False) for relay in pass_relays]
        + [(first, relay, True) for relay in term_relays]
        + [(last, relay, False) for relay in term_relays]
    ):
        greetings.setdefault(here, []).append((there, far))
        if here != there:
            greetings.setdefault(there, []).append((here, far))

    barrier = pltpu.get_barrier_semaphore()

    def greet(device):
        pl.semaphore_signal(barrier, inc=1, device_id=device, device_id_type=MESH)

    for device in [following, previous] + [{"pw": peer} for peer in peers]:
        greet(device)
    callers = 2 + len(peers)
    for here, others in greetings.items():
        callers = callers + len(others) * (spot == here).astype(jnp.int32)

        @pl.when(spot == here)
        def _():
            for other, far in others:
                greet({"band": (across if far else base) + other})

    pl.semaphore_wait(barrier, callers)

    def part(q):
        return pl.ds(q * PART, PART)

    def routes(source, target, relay, send, recv, relay_sends, relay_recvs, onward, ways, end):
        direct, there, then, taken = {}, {}, {}, {}
        for j in range(2):
            for q in range(PARTS):
                direct[j, q] = pltpu.make_async_remote_copy(
                    src_ref=source.at[j, part(q)], dst_ref=target.at[j, part(q)],
                    send_sem=send.at[j], recv_sem=recv.at[j, q // 4],
                    device_id=onward, device_id_type=MESH,
                )
                spot_of = ways[j, q]
                if spot_of is None:
                    continue
                slot = taken.get(spot_of, 0)
                taken[spot_of] = slot + 1
                there[j, q] = pltpu.make_async_remote_copy(
                    src_ref=source.at[j, part(q)], dst_ref=relay.at[slot],
                    send_sem=send.at[j], recv_sem=relay_recvs.at[slot],
                    device_id={"band": across + spot_of}, device_id_type=MESH,
                )
                then[j, q] = pltpu.make_async_remote_copy(
                    src_ref=relay.at[slot], dst_ref=target.at[j, part(q)],
                    send_sem=relay_sends.at[slot], recv_sem=recv.at[j, q // 4],
                    device_id={"band": base + end}, device_id_type=MESH,
                )
        return direct, there, then

    pass_direct, pass_there, pass_then = routes(
        orbitals_in, passing, pass_relay, pass_send, pass_recv,
        relay_send.at[0], relay_recv.at[0], following, pass_routes, first,
    )
    term_direct, term_there, term_then = routes(
        theirs, returned, term_relay, term_send, term_recv,
        relay_send.at[1], relay_recv.at[1], previous, term_routes, last,
    )

    def start(direct, there, source, parts):
        @pl.when(spot == source)
        def _():
            for where in parts:
                there.get(where, direct[where]).start()

        @pl.when(spot != source)
        def _():
            for where in parts:
                direct[where].start()

    def relay_on(there, then, ways, parts):
        for relay in sorted({ways[where] for where in parts if where in then}):

            @pl.when(spot == relay)
            def _():
                for where in parts:
                    if ways[where] == relay:
                        there[where].wait_recv()
                        then[where].start()

    def relay_end(then, ways):
        for relay in sorted({ways[where] for where in then}):

            @pl.when(spot == relay)
            def _():
                for where, copy in then.items():
                    if ways[where] == relay:
                        copy.wait_send()

    def parts_of(j, h=None):
        return [(j, q) for q in range(PARTS) if h is None or q // 4 == h]

    def arrived(ref, sem):
        pltpu.make_async_copy(ref, ref, sem).wait()

    weight_pass = pltpu.make_async_remote_copy(
        src_ref=weights, dst_ref=passed_weights, send_sem=weight_send, recv_sem=weight_recv,
        device_id=following, device_id_type=MESH,
    )

    start(pass_direct, pass_there, last, parts_of(0))
    relay_on(pass_there, pass_then, pass_routes, parts_of(0))
    start(pass_direct, pass_there, last, parts_of(1))
    for copy in inputs:
        copy.wait()
    for i in range(2):
        weight = occupations[i].astype(jnp.float32) * (-0.5 * MIXING)
        weights[i] = jnp.full((8, N), weight, jnp.float32)
    weight_pass.start()

    def slab(index):
        return pl.ds(pl.multiple_of(index * SLAB, SLAB), SLAB)

    def half(h):
        return pl.ds(h * ROWS, ROWS)

    def half_of(index, h):
        return pl.ds(pl.multiple_of(index * SLAB + h * ROWS, ROWS), ROWS)

    def go(p, h):
        pltpu.make_async_copy(
            sent.at[p, slab(place), half(h)], middle.at[p, :, half_of(place, h)], go_recv.at[p]
        ).start()
        for peer in peers:
            pltpu.make_async_remote_copy(
                src_ref=sent.at[p, slab(peer), half(h)],
                dst_ref=middle.at[p, :, half_of(place, h)],
                send_sem=go_send.at[p], recv_sem=go_recv.at[p],
                device_id={"pw": peer}, device_id_type=MESH,
            ).start()

    def come(p, h):
        pltpu.make_async_copy(
            middle.at[p, :, half_of(place, h)], back.at[p, slab(place), half(h)],
            come_recv.at[p, h],
        ).start()
        for peer in peers:
            pltpu.make_async_remote_copy(
                src_ref=middle.at[p, :, half_of(peer, h)],
                dst_ref=back.at[p, slab(place), half(h)],
                send_sem=come_send.at[p], recv_sem=come_recv.at[p, h],
                device_id={"pw": peer}, device_id_type=MESH,
            ).start()

    def forward(i, j, p, h):
        @pl.loop(0, ROWS // 4)
        def _(quad):
            for r in range(2):
                at = pl.ds(h * ROWS + quad * 4 + r * 2, 2)
                field = (orbitals[i, at] * passing[j, at]).reshape(2 * N, N)
                field = from_right(field, table[0])
                field = from_left(table[1], side_by_side(field))
                turned[quad * 4 + r * 2] = field[:, :N]
                turned[quad * 4 + r * 2 + 1] = field[:, N:]

        @pl.loop(0, N // 16)
        def _(block):
            for b in range(2):
                rows = pl.ds(pl.multiple_of(block * 16 + b * 8, 8), 8)
                sent[p, rows, half(h)] = jnp.swapaxes(turned[:, rows], 0, 1)

    for j in range(2):
        for h in range(HALVES):
            arrived(passing.at[j, half(h)], pass_recv.at[j, h])
            for i in range(2):
                forward(i, j, 2 * j + i, h)
                go(2 * j + i, h)
        if j == 0:
            wave_x, share_x = wave_numbers(lax.broadcasted_iota(jnp.int32, (N, N), 0))
            wave_z, share_z = wave_numbers(lax.broadcasted_iota(jnp.int32, (N, N), 1))
            square_xz = wave_x + wave_z
            share_xz = share_x * share_z

            @pl.loop(0, SLAB)
            def _(y):
                wave_y, share_y = wave_numbers(
                    jnp.full((N, N), place * SLAB + y, jnp.int32)
                )
                square = square_xz + wave_y
                safe = jnp.where(square > 0, square, 1.0)
                factor = (4.0 * np.pi) * (share_xz * share_y)
                coulomb[y] = jnp.where(square > 0, factor / safe, 0.0)

    relay_on(pass_there, pass_then, pass_routes, parts_of(1))

    for p in range(4):
        arrived(middle.at[p], go_recv.at[p])

        @pl.loop(0, SLAB // 4)
        def _(quad):
            for r in range(2):
                y = quad * 4 + r * 2
                field = jnp.concatenate([middle[p, y], middle[p, y + 1]], axis=1)
                field = from_left(table[1], field)
                field = field * jnp.concatenate([coulomb[y], coulomb[y + 1]], axis=1)
                field = from_left(table[2], field)
                middle[p, y] = field[:, :N]
                middle[p, y + 1] = field[:, N:]

        come(p, 0)
    core = lax.rem(band, 2)

    @pl.when(core == 0)
    def _():
        for p in range(4):
            come(p, 1)

    for p in range(4):
        if TURNS[p] is None:
            pl.when(core == 1)(functools.partial(come, p, 1))

    weight_pass.wait_recv()
    for h in range(HALVES):
        for j in range(2):
            for i in range(2):
                p = 2 * j + i
                if (h, p) == (1, 2):
                    relay_on(term_there, term_then, term_routes, parts_of(0, 0) + parts_of(1, 0))
                for late in range(4):
                    if TURNS[late] == (h, p):

                        @pl.when(core == 1)
                        def _():
                            pl.semaphore_wait(turn, 1)
                            come(late, 1)

                arrived(back.at[p, :, half(h)], come_recv.at[p, h])
                for late in range(4):
                    if TURNS[late] == (h, p):

                        @pl.when(core == 0)
                        def _():
                            pl.semaphore_signal(
                                turn, inc=1, device_id=following, device_id_type=MESH
                            )


                @pl.loop(0, N // 16)
                def _(block):
                    for b in range(2):
                        rows = pl.ds(pl.multiple_of(block * 16 + b * 8, 8), 8)
                        turned[:, rows] = jnp.swapaxes(back[p, rows, half(h)], 0, 1)

                def backward(quad):
                    for r in range(2):
                        y = quad * 4 + r * 2
                        field = jnp.concatenate([turned[y], turned[y + 1]], axis=1)
                        field = from_left(table[2], field)
                        field = from_right(stacked(field), table[3])
                        potential = field.reshape(2, N // 8, 8, N)
                        at = pl.ds(h * ROWS + y, 2)
                        mine = (
                            potential * passing[j, at].reshape(2, N // 8, 8, N) * passed_weights[j]
                        ).reshape(2, N, N)
                        other = (
                            potential * orbitals[i, at].reshape(2, N // 8, 8, N) * weights[i]
                        ).reshape(2, N, N)
                        if j == 0:
                            out[i, at] = mine
                        else:
                            out[i, at] += mine
                        if i == 0:
                            theirs[j, at] = other
                        else:
                            theirs[j, at] += other

                if i == 0:
                    pl.loop(0, ROWS // 4)(backward)
                else:
                    for quad in range(ROWS // 4):
                        backward(quad)
                        q = 4 * h + 2 * quad
                        start(term_direct, term_there, first, [(j, q), (j, q + 1)])

    relay_on(term_there, term_then, term_routes, parts_of(0, 1) + parts_of(1, 1))
    for h in range(HALVES):
        for j in range(2):
            arrived(returned.at[j, half(h)], term_recv.at[j, h])

            @pl.loop(0, ROWS)
            def _(row):
                out[j, h * ROWS + row] += returned[j, h * ROWS + row]

    relay_end(pass_then, pass_routes)
    relay_end(term_then, term_routes)
    weight_pass.wait_send()
    for j in range(2):
        arrived(passing.at[j], pass_send.at[j])
        arrived(theirs.at[j], term_send.at[j])
    for p in range(4):
        others = pl.ds(0, N - SLAB)
        arrived(sent.at[p, others], go_send.at[p])
        arrived(back.at[p, others], come_send.at[p])


def shards(orbitals, occupations):
    vmem = pl.BlockSpec(memory_space=pltpu.VMEM)
    dma = pltpu.SemaphoreType.DMA
    hbm = pl.BlockSpec(memory_space=pltpu.HBM)
    return pl.pallas_call(
        kernel,
        out_shape=jax.ShapeDtypeStruct(orbitals.shape, jnp.float32),
        in_specs=[hbm, hbm, hbm],
        out_specs=vmem,
        scratch_shapes=[
            pltpu.SMEM(occupations.shape, jnp.int32),
            pltpu.VMEM(orbitals.shape, jnp.float32),
            pltpu.VMEM((4, 2 * N, 2 * N), jnp.bfloat16),
            pltpu.VMEM(orbitals.shape, jnp.float32),
            pltpu.VMEM((2, 8, N), jnp.float32),
            pltpu.VMEM((2, 8, N), jnp.float32),
            pltpu.VMEM((4, N, SLAB, N), jnp.float32),
            pltpu.VMEM((4, SLAB, N, N), jnp.float32),
            pltpu.VMEM((4, N, SLAB, N), jnp.float32),
            pltpu.VMEM(orbitals.shape, jnp.float32),
            pltpu.VMEM(orbitals.shape, jnp.float32),
            pltpu.VMEM((SLAB, N, N), jnp.float32),
            pltpu.VMEM((ROWS, N, N), jnp.float32),
            pltpu.VMEM((PARTS, PART, N, N), jnp.float32),
            pltpu.VMEM((PARTS, PART, N, N), jnp.float32),
            dma((3,)), dma((2,)), dma((2, HALVES)), dma, dma, dma((4,)), dma((4,)), dma((4,)),
            dma((4, HALVES)), dma((2,)), dma((2, HALVES)), dma((2, PARTS)), dma((2, PARTS)),
            pltpu.SemaphoreType.REGULAR,
        ],
        compiler_params=pltpu.CompilerParams(
            collective_id=0, has_side_effects=True, vmem_limit_bytes=48 * 1024 * 1024
        ),
        name="exchange",
    )(*(
        pltpu.with_memory_space_constraint(operand, pltpu.HBM)
        for operand in (occupations, orbitals, jnp.asarray(tables()))
    ))


def solution(mesh):
    placed = (P("band", "pw", None, None), P("band"))
    return jax.shard_map(
        shards, mesh=mesh, in_specs=placed, out_specs=P("band", "pw", None, None), check_vma=False
    )
```

time: 148 us -> 124 us (0.84)
  the two profiles are of different devices: /device:TPU:8 before, /device:TPU:153 now
where the time goes in v3:
time: 124 us
  Pallas kernels  122 us (98%)
  local copies, waits for them, and re-layouts  1.32 us (1%)
    pallas_call x1, Pallas kernels, shards(): pl.pallas_call(kernel, out_shape=jax.ShapeDtypeStruct(orbitals.shape, jnp...  122 us

profile of v3, /device:TPU:153, one launch (start us, length us, event | category | flops | bytes accessed | tf_op | source)
XLA Modules:
  0.0 123.6 jit_solution(11625052249168574137)
XLA Ops:
  0.0 122.3 %exchange.1 = f32[2,16,128,128]{3,2,1,0:T(8,128)S(1)} custom-call(s32[2]{0:T(128)} %occupations_in.1, f32[2,16,128,128]{3,2,1,0:T(8,128)} %orbitals_in.1, bf16[4,256,256]{2,1,0:T(8,128)(2,1)} %constant.2.clone.table_in), custom_call_target="tpu_custom_call" | custom-call | tf_op jit(solution)/shard_map/exchange/pallas_call | solution.py:418
  122.3 1.3 %copy.5 = f32[2,16,128,128]{3,2,1,0:T(8,128)} copy(f32[2,16,128,128]{3,2,1,0:T(8,128)S(1)} %exchange.1) | data formatting | bytes 4194304

commit v4 on v3

--- a/solution.py
+++ b/solution.py
@@ -17,7 +17,8 @@
 MESH = pl.DeviceIdType.MESH
 FAR_FIRST = ((2, 1), (2, 0), (1, 1), (3, 1), (0, 1), (1, 0), (3, 0))
 PARTS = 8
-TURNS = ((0, 0), (0, 1), (0, 2), (0, 3))
+FIRST_TURNS = (None, None, None, 2)
+TURNS = ((0, 3), (1, 0), (1, 1), (1, 2))
 PART = SLAB // PARTS
 
 
@@ -98,12 +99,13 @@
         lax.rem(place_y + dy, 2) * 4 + lax.rem(place_x + dx, 4) for dx, dy in FAR_FIRST
     ]
     first, last = 0, ring - 1
-    near_pass, near_term = (None, last) * 4, (None, first + 1) * 4
-    far_pass = (3, ring - 3, 5, ring - 5) * 2
+    near_pass, near_term = (None, last, None, last, None, last, 7, 7), (None, first + 1) * 4
+    far_pass = (3, 3, 5, 7, 3, ring - 3, 5, 7)
     far_term = (ring - 3, ring - 5, ring - 7, ring - 5)
+    late_term = ((None, first + 1, first + 1, ring - 7), (None, first + 1, None, first + 1))
     pass_routes = {(j, q): (near_pass, far_pass)[j][q] for j in range(2) for q in range(PARTS)}
     term_routes = {
-        (j, q): (far_term + near_term)[q] for j in range(2) for q in range(PARTS)
+        (j, q): (far_term + late_term[j])[q] for j in range(2) for q in range(PARTS)
     }
     pass_relays = sorted({relay for relay in pass_routes.values() if relay is not None})
     term_relays = sorted({relay for relay in term_routes.values() if relay is not None})
@@ -217,7 +219,8 @@
     )
 
     start(pass_direct, pass_there, last, parts_of(0))
-    relay_on(pass_there, pass_then, pass_routes, parts_of(0))
+    prompt = [where for where in parts_of(0) if pass_routes[where] == last]
+    relay_on(pass_there, pass_then, pass_routes, prompt)
     start(pass_direct, pass_there, last, parts_of(1))
     for copy in inputs:
         copy.wait()
@@ -299,10 +302,21 @@
                 factor = (4.0 * np.pi) * (share_xz * share_y)
                 coulomb[y] = jnp.where(square > 0, factor / safe, 0.0)
 
-    relay_on(pass_there, pass_then, pass_routes, parts_of(1))
-
+    relay_on(
+        pass_there, pass_then, pass_routes,
+        [where for j in range(2) for where in parts_of(j) if where not in prompt],
+    )
+
+    core = lax.rem(band, 2)
     for p in range(4):
         arrived(middle.at[p], go_recv.at[p])
+        signals = FIRST_TURNS.count(p)
+        if signals:
+
+            @pl.when(core == 0)
+            def _():
+                pl.semaphore_signal(turn, inc=signals, device_id=following, device_id_type=MESH)
+
 
         @pl.loop(0, SLAB // 4)
         def _(quad):
@@ -315,8 +329,14 @@
                 middle[p, y] = field[:, :N]
                 middle[p, y + 1] = field[:, N:]
 
+        if FIRST_TURNS[p] is not None:
+
+            @pl.when(core == 1)
+            def _():
+                pl.semaphore_wait(turn, 1)
+
         come(p, 0)
-    core = lax.rem(band, 2)
+
 
     @pl.when(core == 0)
     def _():

time: 124 us -> 118 us (0.952)
  the two profiles are of different devices: /device:TPU:153 before, /device:TPU:1 now
where the time goes in v4:
time: 118 us; the launch traced here: 117 us
  Pallas kernels  116 us (98%)
  local copies, waits for them, and re-layouts  1.32 us (1%)
    pallas_call x1, Pallas kernels, shards(): pl.pallas_call(kernel, out_shape=jax.ShapeDtypeStruct(orbitals.shape, jnp...  116 us

profile of v4, /device:TPU:1, one launch (start us, length us, event | category | flops | bytes accessed | tf_op | source)
XLA Modules:
  0.0 117.4 jit_solution(4424438295134185028)
XLA Ops:
  0.0 116.1 %exchange.1 = f32[2,16,128,128]{3,2,1,0:T(8,128)S(1)} custom-call(s32[2]{0:T(128)} %occupations_in.1, f32[2,16,128,128]{3,2,1,0:T(8,128)} %orbitals_in.1, bf16[4,256,256]{2,1,0:T(8,128)(2,1)} %constant.2.clone.table_in), custom_call_target="tpu_custom_call" | custom-call | tf_op jit(solution)/shard_map/exchange/pallas_call | solution.py:438
  116.1 1.3 %copy.5 = f32[2,16,128,128]{3,2,1,0:T(8,128)} copy(f32[2,16,128,128]{3,2,1,0:T(8,128)S(1)} %exchange.1) | data formatting | bytes 4194304

commit v5 on v4

--- a/solution.py
+++ b/solution.py
@@ -15,7 +15,7 @@
 HALVES = 2
 ROWS = SLAB // HALVES
 MESH = pl.DeviceIdType.MESH
-FAR_FIRST = ((2, 1), (2, 0), (1, 1), (3, 1), (0, 1), (1, 0), (3, 0))
+FAR_FIRST = ((2, 1), (1, 0), (3, 0), (0, 1), (2, 0), (1, 1), (3, 1))
 PARTS = 8
 FIRST_TURNS = (None, None, None, 2)
 TURNS = ((0, 3), (1, 0), (1, 1), (1, 2))

time: 118 us -> 117 us (level)
  no operation moved by 1% of the time
where the time goes in v5:
time: 117 us
  Pallas kernels  116 us (99%)
  local copies, waits for them, and re-layouts  1.32 us (1%)
    pallas_call x1, Pallas kernels, shards(): pl.pallas_call(kernel, out_shape=jax.ShapeDtypeStruct(orbitals.shape, jnp...  116 us

profile of v5, /device:TPU:1, one launch (start us, length us, event | category | flops | bytes accessed | tf_op | source)
XLA Modules:
  0.0 117.4 jit_solution(9201669000024779774)
XLA Ops:
  0.0 116.1 %exchange.1 = f32[2,16,128,128]{3,2,1,0:T(8,128)S(1)} custom-call(s32[2]{0:T(128)} %occupations_in.1, f32[2,16,128,128]{3,2,1,0:T(8,128)} %orbitals_in.1, bf16[4,256,256]{2,1,0:T(8,128)(2,1)} %constant.2.clone.table_in), custom_call_target="tpu_custom_call" | custom-call | tf_op jit(solution)/shard_map/exchange/pallas_call | solution.py:438
  116.1 1.3 %copy.5 = f32[2,16,128,128]{3,2,1,0:T(8,128)} copy(f32[2,16,128,128]{3,2,1,0:T(8,128)S(1)} %exchange.1) | data formatting | bytes 4194304

commit v6 on v5

--- a/solution.py
+++ b/solution.py
@@ -102,7 +102,7 @@
     near_pass, near_term = (None, last, None, last, None, last, 7, 7), (None, first + 1) * 4
     far_pass = (3, 3, 5, 7, 3, ring - 3, 5, 7)
     far_term = (ring - 3, ring - 5, ring - 7, ring - 5)
-    late_term = ((None, first + 1, first + 1, ring - 7), (None, first + 1, None, first + 1))
+    late_term = ((first + 1, ring - 7, first + 1, None), (first + 1, first + 1, None, None))
     pass_routes = {(j, q): (near_pass, far_pass)[j][q] for j in range(2) for q in range(PARTS)}
     term_routes = {
         (j, q): (far_term + late_term[j])[q] for j in range(2) for q in range(PARTS)

time: 117 us -> 117 us (level)
  no operation moved by 1% of the time
where the time goes in v6:
time: 117 us
  Pallas kernels  116 us (99%)
  local copies, waits for them, and re-layouts  1.32 us (1%)
    pallas_call x1, Pallas kernels, shards(): pl.pallas_call(kernel, out_shape=jax.ShapeDtypeStruct(orbitals.shape, jnp...  116 us

profile of v6, /device:TPU:1, one launch (start us, length us, event | category | flops | bytes accessed | tf_op | source)
XLA Modules:
  0.0 117.4 jit_solution(1207008959214391731)
XLA Ops:
  0.0 116.1 %exchange.1 = f32[2,16,128,128]{3,2,1,0:T(8,128)S(1)} custom-call(s32[2]{0:T(128)} %occupations_in.1, f32[2,16,128,128]{3,2,1,0:T(8,128)} %orbitals_in.1, bf16[4,256,256]{2,1,0:T(8,128)(2,1)} %constant.2.clone.table_in), custom_call_target="tpu_custom_call" | custom-call | tf_op jit(solution)/shard_map/exchange/pallas_call | solution.py:438
  116.1 1.3 %copy.5 = f32[2,16,128,128]{3,2,1,0:T(8,128)} copy(f32[2,16,128,128]{3,2,1,0:T(8,128)S(1)} %exchange.1) | data formatting | bytes 4194304
